TPU v7x, 512 devices: a whole 4x8x8 slice. The times are simulated.
512 devices in a mesh: vocab: 64 (over y, z_lo, core), batch: 8 (over z_hi, x).
Axes of the slice: x: 4, y: 8, z: 8 (z_hi: 2, z_lo: 4; z = z_hi * 4 + z_lo), core: 2. Of those that a mesh axis runs over, the one named last changes fastest.
Arguments:
- latent_states: bfloat16 [128, 5, 16384], P('vocab', None, 'batch'), may hold values from -150 to 150
- unembedding_weights: bfloat16 [16384, 8, 64, 128], P('batch', None, 'vocab'), may hold values from -0.046875 to 0.046875
- drafter_raw_scores: bfloat16 [128, 5, 8, 64, 128], P('vocab', None, 'batch'), may hold values from -16 to 160
- sampler_heat: float32 [128], P('batch'), may hold values from 0.7 to 1.4
- drafter_guesses: int32 [128, 5], P('batch'), may hold values from 0 to 65535
- first_refused_slot: int32 [128], P('batch'), may hold values from 0 to 4
Outputs:
- ratio: float32 [128, 5], P('batch')
- residual: bfloat16 [128, 8, 64, 128], P('batch', None, 'vocab')
All inputs are finite; a program needn't handle non-finite values.
Results may differ from a plain program's by a relative error of at most 0.01105.
Values may be sent and summed in bfloat16 or wider, within the bound.
A program may use at most 64 MiB of HBM per device.

v0:
```python
import jax
import jax.numpy as jnp
from jax import lax
from jax.sharding import PartitionSpec as P

blend_share = 0.0625


def per_device(
    latent_states,
    unembedding_weights,
    drafter_raw_scores,
    sampler_heat,
    drafter_guesses,
    first_refused_slot,
):
    depth = latent_states.shape[2]
    outer_count = unembedding_weights.shape[1]
    lane_width = unembedding_weights.shape[3]
    columns = outer_count * lane_width
    weight_block = unembedding_weights.reshape(depth, columns)
    queries_within_bundle = sampler_heat.shape[0]
    positions = drafter_guesses.shape[1]
    gathered = lax.all_gather(latent_states, "vocab", axis=0, tiled=True)
    every_row = gathered.reshape(-1, depth)
    logits = lax.psum_scatter(
        jnp.dot(every_row, weight_block, preferred_element_type=jnp.float32),
        "batch",
        scatter_dimension=0,
        tiled=True,
    )
    multiplier = sampler_heat[:, None, None]
    target_scores = logits.reshape(queries_within_bundle, positions, columns) / multiplier
    relaid = lax.all_to_all(
        lax.all_to_all(drafter_raw_scores, "vocab", split_axis=3, concat_axis=0, tiled=True),
        "batch",
        split_axis=0,
        concat_axis=2,
        tiled=True,
    )
    draft_scores = (
        relaid.reshape(queries_within_bundle, positions, columns).astype(jnp.float32) / multiplier
    )
    target_max, draft_max = lax.pmax(
        (jnp.max(target_scores, axis=-1), jnp.max(draft_scores, axis=-1)), "vocab"
    )
    target_exp = jnp.exp(target_scores - target_max[..., None])
    draft_exp = jnp.exp(draft_scores - draft_max[..., None])
    target_total, draft_total = lax.psum(
        (jnp.sum(target_exp, axis=-1), jnp.sum(draft_exp, axis=-1)), "vocab"
    )
    target_prob = target_exp / target_total[..., None]
    draft_prob = draft_exp / draft_total[..., None]
    vocab_index = lax.axis_index("vocab")
    vocab_count = lax.axis_size("vocab")
    outer_ids = lax.broadcasted_iota(jnp.int32, (outer_count, lane_width), 0)
    inner_ids = lax.broadcasted_iota(jnp.int32, (outer_count, lane_width), 1)
    token_ids = ((outer_ids * vocab_count + vocab_index) * lane_width + inner_ids).reshape(columns)
    matches = token_ids[None, None, :] == drafter_guesses[..., None]
    target_hit = jnp.sum(jnp.where(matches, target_scores, 0.0), axis=-1)
    draft_hit = jnp.sum(jnp.where(matches, draft_scores, 0.0), axis=-1)
    chosen_step = (
        lax.broadcasted_iota(jnp.int32, (queries_within_bundle, positions), 1)
        == first_refused_slot[:, None]
    )
    target_stop = jnp.sum(jnp.where(chosen_step[..., None], target_prob, 0.0), axis=1)
    draft_stop = jnp.sum(jnp.where(chosen_step[..., None], draft_prob, 0.0), axis=1)
    excess = jnp.maximum(target_stop - draft_stop, 0.0) + blend_share * target_stop
    target_token, draft_token, excess_total = lax.psum(
        (target_hit, draft_hit, jnp.sum(excess, axis=-1)), "vocab"
    )
    target_log = target_token - target_max - jnp.log(target_total)
    draft_log = draft_token - draft_max - jnp.log(draft_total)
    ratio = jnp.exp(jnp.minimum(0.0, target_log - draft_log))
    residual = (excess / excess_total[:, None]).astype(jnp.bfloat16)
    residual = residual.reshape(queries_within_bundle, outer_count, 1, lane_width)
    return (ratio, residual)


def solution(mesh):
    in_specs = (
        P("vocab", None, "batch"),
        P("batch", None, "vocab", None),
        P("vocab", None, "batch", None, None),
        P("batch"),
        P("batch", None),
        P("batch"),
    )
    out_specs = (P("batch", None), P("batch", None, "vocab", None))
    return jax.shard_map(
        per_device, mesh=mesh, in_specs=in_specs, out_specs=out_specs, check_vma=False
    )
```

profile of v0, /device:TPU:1, one launch (start us, length us, event | category | flops | bytes accessed | tf_op | source)
XLA Modules:
  0.0 680.7 jit_solution(1210893383195697851)
XLA Ops:
  7.2 0.0 all-gather.2.cloned.1.call-start
  7.2 1.4 copy.51
  8.6 0.0 all-gather.2.cloned.1.call-update
  8.7 0.0 reduce-scatter.2.cloned.1.call-start
  8.7 127.9 %all-gather.2.cloned.1.call-done = bf16[128,5,2048]{2,1,0:T(8,128)(2,1)} async-done(((bf16[2,5,2048]{2,1,0:T(8,128)(2,1)}), bf16[128,5,2048]{2,1,0:T(8,128)(2,1)}) %all-gather.2.cloned.1.call-update) | async-done | bytes 2621456 | tf_op jit(solution)/shard_map/all_gather | solution.py:24
  136.6 4.2 reshape.138
  140.8 0.0 copy-start
  140.8 0.0 copy-start.2
  140.8 0.0 copy-start.1
  140.8 6.6 fusion
  147.5 0.0 reduce-scatter.2.cloned.1.call-update
  147.5 0.8 copy.56
  148.4 7.1 %all-to-all-start = ((bf16[2,5,1,64,128]{4,1,2,0,3:T(8,128)(2,1)}), bf16[2,5,1,64,128]{4,1,2,0,3:T(8,128)(2,1)S(1)}, u32[]{:S(2)}, u32[]{:S(2)}) async-start(bf16[2,5,1,64,128]{4,1,2,0,3:T(8,128)(2,1)} %copy.56), calls=%async_computation.1 | async-start | bytes 524288 | tf_op jit(solution)/shard_map/all_to_all | solution.py:35
  155.5 0.1 div.66
  155.6 0.1 div.67
  155.7 0.1 copy.50
  155.7 0.1 eq.42
  155.9 0.1 copy.61
  156.0 12.6 %all-to-all-done = bf16[2,5,1,64,128]{4,1,2,0,3:T(8,128)(2,1)S(1)} async-done(((bf16[2,5,1,64,128]{4,1,2,0,3:T(8,128)(2,1)}), bf16[2,5,1,64,128]{4,1,2,0,3:T(8,128)(2,1)S(1)}, u32[]{:S(2)}, u32[]{:S(2)}) %all-to-all-start) | async-done | bytes 163872 | tf_op jit(solution)/shard_map/all_to_all | solution.py:35
  168.6 0.2 copy.58
  168.7 0.8 copy.59
  169.6 7.0 %all-to-all-start.1 = ((bf16[128,5,1,1,128]{4,1,3,2,0:T(8,128)(2,1)}), bf16[128,5,1,1,128]{4,1,3,2,0:T(8,128)(2,1)S(1)}, u32[]{:S(2)}, u32[]{:S(2)}) async-start(bf16[128,5,1,1,128]{4,1,3,2,0:T(8,128)(2,1)} %copy.59), calls=%async_computation.2 | async-start | bytes 524288 | tf_op jit(solution)/shard_map/all_to_all | solution.py:34
  176.6 0.1 iota_add_fusion
  176.6 10.8 %all-to-all-done.1 = bf16[128,5,1,1,128]{4,1,3,2,0:T(8,128)(2,1)S(1)} async-done(((bf16[128,5,1,1,128]{4,1,3,2,0:T(8,128)(2,1)}), bf16[128,5,1,1,128]{4,1,3,2,0:T(8,128)(2,1)S(1)}, u32[]{:S(2)}, u32[]{:S(2)}) %all-to-all-start.1) | async-done | bytes 163872 | tf_op jit(solution)/shard_map/all_to_all | solution.py:34
  187.5 0.2 fusion.14
  187.7 68.6 %reduce-scatter.2.cloned.1.call-done = f32[80,1024]{1,0:T(8,128)} async-done(((f32[640,1024]{1,0:T(8,128)}), f32[80,1024]{1,0:T(8,128)}) %reduce-scatter.2.cloned.1.call-update) | async-done | bytes 327696 | tf_op jit(solution)/shard_map/reduce_scatter | solution.py:26
  256.2 1.2 select_reduce_fusion.3
  257.4 0.1 reduce_max.21
  257.5 0.1 copy.53
  257.6 137.0 %all-reduce.2 = (f32[16,5]{0,1:T(8,128)S(1)}, f32[16,5]{0,1:T(8,128)S(1)}) all-reduce(f32[16,5]{0,1:T(8,128)S(1)} %fusion.14, f32[16,5]{0,1:T(8,128)S(1)} %copy.53), channel_id=1, replica_groups=mesh['vocab'=64,'batch'=8] {'vocab'}, use_global_device_ids=true, to_apply=%region_10.11 | all-reduce | flops 160 | bytes 1280 | tf_op jit(solution)/shard_map/pmax | solution.py:44
  394.6 0.1 copy.54
  394.7 0.1 sub.59
  394.8 1.2 exponential_reduce_fusion
  396.0 0.1 reduce_sum.76
  396.1 0.1 copy.55
  396.2 0.2 fusion.4
  396.4 136.8 %all-reduce.1 = (f32[16,5]{0,1:T(8,128)S(1)}, f32[16,5]{0,1:T(8,128)S(1)}) all-reduce(f32[16,5]{0,1:T(8,128)S(1)} %fusion.4, f32[16,5]{0,1:T(8,128)S(1)} %copy.55), channel_id=1, replica_groups=mesh['vocab'=64,'batch'=8] {'vocab'}, use_global_device_ids=true, to_apply=%region_12.13 | all-reduce | flops 160 | bytes 1280 | tf_op jit(solution)/shard_map/psum | solution.py:49
  533.2 0.1 copy.63
  533.3 0.1 reduce_sum.74
  533.4 0.1 copy.52
  533.4 0.2 select_reduce_fusion.1
  533.7 1.0 reshape.140
  534.7 0.3 select_reduce_fusion
  535.0 0.1 fusion.7
  535.2 137.3 %all-reduce = (f32[16,5]{0,1:T(8,128)S(1)}, f32[16,5]{0,1:T(8,128)S(1)}, f32[16]{0:T(128)S(1)}) all-reduce(f32[16,5]{0,1:T(8,128)S(1)} %get-tuple-element.15, f32[16,5]{0,1:T(8,128)S(1)} %copy.52, f32[16]{0:T(128)S(1)} %fusion.7), channel_id=1, replica_groups=mesh['vocab'=64,'batch'=8] {'vocab'}, use_global_device_ids=true, to_apply=%region_8.0 | all-reduce | flops 176 | bytes 1408 | tf_op jit(solution)/shard_map/psum | solution.py:69
  672.6 0.1 fusion.11
  672.6 0.6 copy.67
  673.3 0.6 minimum_exponential_fusion
  (10 shorter events, 0.1 us)
Async XLA Ops:
  7.2 129.4 %all-gather.2.cloned.1.call-start = ((), (), s32[]{:S(2)}) async-start(), calls=%async_computation.3 | async-start | bytes 4259840 | tf_op jit(solution)/shard_map/all_gather | solution.py:24
  8.7 247.6 %reduce-scatter.2.cloned.1.call-start = ((), (), s32[]{:S(2)}) async-start(), calls=%async_computation.4 | async-start | bytes 2949120 | tf_op jit(solution)/shard_map/reduce_scatter | solution.py:26
  140.8 6.7 copy-start
  140.8 14.7 %copy-start.2 = (f32[16]{0:T(128)S(1)}, f32[16]{0:T(128)}, u32[]{:S(2)}) copy-start(f32[16]{0:T(128)} %param.9) | copy-start | bytes 196
  140.8 14.8 %copy-start.1 = (s32[16,5]{0,1:T(8,128)S(1)}, s32[16,5]{0,1:T(8,128)}, u32[]{:S(2)}) copy-start(s32[16,5]{0,1:T(8,128)} %param.10) | copy-start | bytes 964
  140.8 15.0 %copy-start.3 = (s32[16]{0:T(128)S(1)}, s32[16]{0:T(128)}, u32[]{:S(2)}) copy-start(s32[16]{0:T(128)} %param.11) | copy-start | bytes 196
  148.4 20.1 %all-to-all-start = ((bf16[2,5,1,64,128]{4,1,2,0,3:T(8,128)(2,1)}), bf16[2,5,1,64,128]{4,1,2,0,3:T(8,128)(2,1)S(1)}, u32[]{:S(2)}, u32[]{:S(2)}) async-start(bf16[2,5,1,64,128]{4,1,2,0,3:T(8,128)(2,1)} %copy.56), calls=%async_computation.1 | async-start | bytes 524288 | tf_op jit(solution)/shard_map/all_to_all | solution.py:35
  169.6 17.9 %all-to-all-start.1 = ((bf16[128,5,1,1,128]{4,1,3,2,0:T(8,128)(2,1)}), bf16[128,5,1,1,128]{4,1,3,2,0:T(8,128)(2,1)S(1)}, u32[]{:S(2)}, u32[]{:S(2)}) async-start(bf16[128,5,1,1,128]{4,1,3,2,0:T(8,128)(2,1)} %copy.59), calls=%async_computation.2 | async-start | bytes 524288 | tf_op jit(solution)/shard_map/all_to_all | solution.py:34
Sparse Core Ops, SparseCore 0:
  10.1 126.4 all-gather.1
  147.6 108.5 reduce-scatter.1
where the time goes:
time: 681 us
  blocking collectives  411 us (60%)
  waiting for transfers between devices  220 us (32%)
  starting transfers between devices  14.2 us (2%)
  between operations  14.2 us (2%)
  local copies, waits for them, and re-layouts  10.4 us (2%)
    psum x1, blocking collectives, per_device(): lax.psum((target_hit, draft_hit, jnp.sum(excess, axis=-1)), 'vocab')  137 us
    pmax x1, blocking collectives, per_device(): lax.pmax((jnp.max(target_scores, axis=-1), jnp.max(draft_scores, axis=-1)...  137 us
    psum x1, blocking collectives, per_device(): lax.psum((jnp.sum(target_exp, axis=-1), jnp.sum(draft_exp, axis=-1)), 'vo...  137 us
    all_gather x1, waiting for transfers between devices, per_device(): gathered = lax.all_gather(latent_states, 'vocab', axis=0, tiled=True)  128 us
    reduce_scatter x1, waiting for transfers between devices, per_device(): lax.psum_scatter(jnp.dot(every_row, weight_block, preferred_element_type=...  68.6 us
  transfers between devices with their start and end apart: 4, of which 4 were waited for; matrix products, arithmetic and copies ran while one was open for 0% of the time, Pallas kernels for 0%

commit v1 on v0

v1 whole, which is shorter than its diff:
```python
import jax
import jax.numpy as jnp
from jax import lax
from jax.experimental import pallas as pl
from jax.experimental.pallas import tpu as pltpu
from jax.sharding import PartitionSpec as P

blend_share = 0.0625

RING_Y = 8
GROUP = 8
RING_X = 4
REQ = 2
POS = 5
LANE = 128
MESH = pl.DeviceIdType.MESH
OFFSETS = ((0,), (-1, 1), (-2, 2), (-3, 3), (4,))


def kernel(
    x_ref,
    w_hbm,
    d_ref,
    meta_ref,
    ratio_ref,
    resid_ref,
    w_raw,
    w_mat,
    z_in,
    g,
    part,
    relay_in,
    root_in,
    cross_in,
    a1,
    a2,
    a3,
    ts,
    ds,
    st_out,
    st_in,
    w_sem,
    z_send,
    z_recv,
    y_send,
    y_recv,
    sib_send,
    sib_recv,
    p_send,
    relay_recv,
    root_recv,
    cross_recv,
    a_send,
    a_recv,
    st_send,
    st_recv,
):
    v = lax.axis_index("vocab")
    b = lax.axis_index("batch")
    y = v // GROUP
    place = v % GROUP
    core = place % 2
    x = b % RING_X
    zh = b // RING_X
    depth = w_raw.shape[0]
    chunks = x_ref.shape[1]
    half_chunks = chunks // 2
    rows = meta_ref.shape[0]
    outer = w_raw.shape[1]
    columns = outer * LANE
    half = columns // 2
    queries = rows // POS

    def at(y_, place_, b_):
        return (y_ * GROUP + place_, b_)

    def remote(src, dst, send, recv, device):
        return pltpu.make_async_remote_copy(
            src_ref=src,
            dst_ref=dst,
            send_sem=send,
            recv_sem=recv,
            device_id=device,
            device_id_type=MESH,
        )

    def await_bytes(ref, sem):
        pltpu.make_async_copy(ref, ref, sem).wait()

    w_copy = pltpu.make_async_copy(w_hbm, w_raw, w_sem)
    w_copy.start()

    barrier = pltpu.get_barrier_semaphore()
    for t in range(1, 8):
        pl.semaphore_signal(
            barrier, inc=1, device_id=at(y, (place + t) % GROUP, b), device_id_type=MESH
        )
        pl.semaphore_signal(
            barrier, inc=1, device_id=at((y + t) % RING_Y, place, b), device_id_type=MESH
        )
        pl.semaphore_signal(
            barrier, inc=1, device_id=at(y, place, (b + t) % 8), device_id_type=MESH
        )
    pl.semaphore_wait(barrier, 21)

    for t in range(1, 8):
        to = (place + t) % GROUP
        first = (to % 2) * half_chunks
        remote(
            x_ref.at[:, pl.ds(first, half_chunks)],
            z_in.at[place],
            z_send,
            z_recv,
            at(y, to, b),
        ).start()
    pltpu.make_async_copy(
        x_ref.at[:, pl.ds(core * half_chunks, half_chunks)], z_in.at[place], z_recv
    ).start()

    for t in range(1, 8):
        to = (place + t) % GROUP
        remote(
            d_ref.at[:, to], a1.at[place], a_send.at[0], a_recv.at[0], at(y, to, b)
        ).start()
    pltpu.make_async_copy(d_ref.at[:, place], a1.at[place], a_recv.at[0]).start()

    w_copy.wait()
    fold = 64

    @pl.loop(0, depth // fold)
    def _(i):
        f = pl.multiple_of(i * fold, fold)
        w_mat[pl.ds(f, fold), :] = w_raw[pl.ds(f, fold)].reshape(fold, columns)

    def mine(yy):
        return g.at[yy, pl.ds(core * half_chunks, half_chunks)]

    def to_sibling(yy, k):
        remote(
            mine(yy), mine(yy), sib_send.at[k], sib_recv.at[k], at(y, place + 1 - 2 * core, b)
        ).start()

    def theirs(yy):
        return g.at[yy, pl.ds((1 - core) * half_chunks, half_chunks)]

    def wait_sibling(yy, k):
        await_bytes(theirs(yy), sib_recv.at[k])

    right = at((y + 1) % RING_Y, place, b)
    left = at((y + RING_Y - 1) % RING_Y, place, b)

    def around(o):
        return (y + o + RING_Y) % RING_Y

    await_bytes(z_in, z_recv)
    for s in range(half_chunks):
        g[y, core * half_chunks + s] = jnp.swapaxes(z_in[:, :, s], 0, 1).reshape(rows, LANE)
    remote(mine(y), mine(y), y_send.at[0, 0], y_recv.at[0, 0], right).start()
    remote(mine(y), mine(y), y_send.at[1, 0], y_recv.at[1, 0], left).start()
    to_sibling(y, 0)

    await_bytes(a1, a_recv.at[0])
    for t in range(1, 8):
        to = (y + t) % RING_Y
        remote(
            a1.at[:, to], a2.at[y], a_send.at[1], a_recv.at[1], at(to, place, b)
        ).start()
    pltpu.make_async_copy(a1.at[:, y], a2.at[y], a_recv.at[1]).start()

    quarter = half_chunks // 2

    def sub(yy, direction):
        return g.at[yy, pl.ds(core * half_chunks + direction * quarter, quarter)]

    def ring_step(t):
        if t < 4:
            for direction, to in ((0, right), (1, left)):
                yy = around(-t if direction == 0 else t)
                await_bytes(mine(yy), y_recv.at[direction, t - 1])
                piece = mine(yy) if t < 3 else sub(yy, direction)
                remote(
                    piece, piece, y_send.at[direction, t], y_recv.at[direction, t], to
                ).start()
                to_sibling(yy, 2 * t - 1 + direction)
        else:
            yy = around(4)
            for direction in (0, 1):
                await_bytes(sub(yy, direction), y_recv.at[direction, 3])
            to_sibling(yy, 7)

    def multiply(blocks):
        span = 256
        for n in range(columns // span):
            acc = None
            for kk in range(depth // 256):
                lhs = jnp.concatenate(
                    [
                        jnp.concatenate([g[yy, 2 * kk], g[yy, 2 * kk + 1]], axis=1)
                        for yy in blocks
                    ],
                    axis=0,
                )
                term = jnp.dot(
                    lhs,
                    w_mat[kk * 256 : (kk + 1) * 256, n * span : (n + 1) * span],
                    preferred_element_type=jnp.float32,
                )
                acc = term if acc is None else acc + term
            at_half, col = (n * span) // half, (n * span) % half
            for i, yy in enumerate(blocks):
                part[yy, at_half, :, col : col + span] = acc[i * rows : (i + 1) * rows]

    def roles(yy):
        xd = yy % RING_X
        return xd, (x - xd + RING_X) % RING_X, yy // RING_X

    def reduce_a(yy):
        xd, d, rk = roles(yy)

        @pl.when(d == 2)
        def _():
            for h, nb in ((0, (xd + 1) % RING_X), (1, (xd + 3) % RING_X)):
                remote(
                    part.at[yy, h],
                    relay_in.at[yy],
                    p_send.at[yy, h],
                    relay_recv.at[yy],
                    (v, zh * RING_X + nb),
                ).start()

        @pl.when(d % 2 == 1)
        def _():
            side = d // 2
            remote(
                part.at[yy, 1 - side],
                root_in.at[rk, side, 1 - side],
                p_send.at[yy, 1 - side],
                root_recv.at[rk, side, 1 - side],
                (v, zh * RING_X + xd),
            ).start()

    def reduce_b(yy):
        xd, d, rk = roles(yy)

        @pl.when(d % 2 == 1)
        def _():
            side = d // 2
            await_bytes(relay_in.at[yy], relay_recv.at[yy])
            part[yy, side] = part[yy, side] + relay_in[yy]
            remote(
                part.at[yy, side],
                root_in.at[rk, side, side],
                p_send.at[yy, side],
                root_recv.at[rk, side, side],
                (v, zh * RING_X + xd),
            ).start()

    def reduce_c(yy):
        xd, d, rk = roles(yy)

        @pl.when(d == 0)
        def _():
            for h in (0, 1):
                await_bytes(root_in.at[rk, 1 - h, h], root_recv.at[rk, 1 - h, h])
                await_bytes(root_in.at[rk, h, h], root_recv.at[rk, h, h])
                part[yy, h] = part[yy, h] + root_in[rk, 0, h] + root_in[rk, 1, h]

                @pl.when(rk != zh)
                def _():
                    remote(
                        part.at[yy, h],
                        cross_in.at[h],
                        p_send.at[yy, h],
                        cross_recv.at[h],
                        (v, rk * RING_X + x),
                    ).start()

    heat = meta_ref[:, 0:1]
    guess = meta_ref[:, 1:2].astype(jnp.int32)
    stop = meta_ref[:, 2:3]
    lane_ids = lax.broadcasted_iota(jnp.int32, (rows, LANE), 1)

    def statistics(scores):
        top = scores[0]
        for o in range(1, outer):
            top = jnp.maximum(top, scores[o])
        top = jnp.max(top, axis=1, keepdims=True)
        total = jnp.zeros((rows, LANE), jnp.float32)
        hit = jnp.zeros((rows, LANE), jnp.float32)
        for o in range(outer):
            value = scores[o]
            total = total + jnp.exp(value - top)
            ids = (o * (RING_Y * GROUP) + v) * LANE + lane_ids
            hit = hit + jnp.where(ids == guess, value, 0.0)
        return (
            top,
            jnp.sum(total, axis=1, keepdims=True),
            jnp.sum(hit, axis=1, keepdims=True),
        )

    def draft_scores():
        await_bytes(a3, a_recv.at[2])
        for o in range(outer):
            logits = jnp.swapaxes(a3[o], 0, 1).reshape(rows, LANE).astype(jnp.float32)
            ds[o] = logits / heat
        return statistics(ds)

    def draft_step_3():
        await_bytes(a2, a_recv.at[1])
        for t in range(1, 8):
            to = (b + t) % 8
            remote(a2.at[to], a3.at[b], a_send.at[2], a_recv.at[2], at(y, place, to)).start()
        pltpu.make_async_copy(a2.at[b], a3.at[b], a_recv.at[2]).start()

    ring_step(1)
    wait_sibling(y, 0)
    multiply((y,))
    reduce_a(y)
    draft_step_3()

    ring_step(2)
    wait_sibling(around(-1), 1)
    wait_sibling(around(1), 2)
    multiply((around(-1), around(1)))
    reduce_a(around(-1))
    reduce_a(around(1))
    reduce_b(y)

    ring_step(3)
    wait_sibling(around(-2), 3)
    wait_sibling(around(2), 4)
    multiply((around(-2), around(2)))
    reduce_a(around(-2))
    reduce_a(around(2))
    reduce_b(around(-1))
    reduce_b(around(1))
    reduce_c(y)

    ring_step(4)
    wait_sibling(around(-3), 5)
    wait_sibling(around(3), 6)
    multiply((around(-3), around(3)))
    reduce_a(around(-3))
    reduce_a(around(3))
    reduce_b(around(-2))
    reduce_b(around(2))
    reduce_c(around(-1))
    reduce_c(around(1))

    wait_sibling(around(4), 7)
    multiply((around(4),))
    reduce_a(around(4))
    reduce_b(around(-3))
    reduce_b(around(3))
    reduce_c(around(-2))
    reduce_c(around(2))
    reduce_b(around(4))
    reduce_c(around(-3))
    reduce_c(around(3))
    d_top, d_total, d_hit = draft_scores()
    reduce_c(around(4))

    for h in (0, 1):
        await_bytes(cross_in.at[h], cross_recv.at[h])
        for i in range(outer // 2):
            span = slice(i * LANE, (i + 1) * LANE)
            ts[h * (outer // 2) + i] = (part[b, h, :, span] + cross_in[h, :, span]) / heat
    t_top, t_total, t_hit = statistics(ts)

    def spread(k, hop):
        me = (place, y)[hop]
        for t in range(1, 8):
            to = (me + t) % 8
            remote(
                st_out.at[k],
                st_in.at[k, me],
                st_send.at[k],
                st_recv.at[k],
                at(y, to, b) if hop == 0 else at(to, place, b),
            ).start()
        pltpu.make_async_copy(st_out.at[k], st_in.at[k, me], st_recv.at[k]).start()
        await_bytes(st_in.at[k], st_recv.at[k])

    wide = jnp.zeros((rows, LANE), jnp.float32)
    for i, column in enumerate((t_top, t_total, t_hit, d_top, d_total, d_hit)):
        wide = jnp.where(lane_ids == i, column, wide)
    wide = jnp.concatenate([wide, jnp.ones((LANE - rows, LANE), jnp.float32)], axis=0)
    st_out[0] = jnp.transpose(wide)[0:8]

    def merged(k):
        out = []
        for i in (0, 3):
            top = st_in[k, 0, i : i + 1]
            for j in range(1, 8):
                top = jnp.maximum(top, st_in[k, j, i : i + 1])
            total = jnp.zeros_like(top)
            hit = jnp.zeros_like(top)
            for j in range(8):
                total = total + st_in[k, j, i + 1 : i + 2] * jnp.exp(
                    st_in[k, j, i : i + 1] - top
                )
                hit = hit + st_in[k, j, i + 2 : i + 3]
            out += [top, total, hit]
        return out

    spread(0, 0)
    for i, value in enumerate(merged(0)):
        st_out[1, i : i + 1] = value
    st_out[1, 6:8] = jnp.zeros((2, LANE), jnp.float32)
    spread(1, 1)
    t_max, t_sum, t_tok, d_max, d_sum, d_tok = merged(1)

    def chosen(block):
        out = None
        for p in range(POS):
            mask = stop[p * queries : (p + 1) * queries] > 0.5
            value = block(p)
            picked = jnp.where(mask, value, 0.0)
            out = picked if out is None else out + picked
        return out

    def rows_of(p):
        return slice(p * queries, (p + 1) * queries)

    filler = jnp.zeros((LANE - 4, LANE), jnp.float32)
    tall = jnp.transpose(jnp.concatenate([t_max, t_sum, d_max, d_sum, filler], axis=0))
    picks = chosen(lambda p: tall[rows_of(p)])
    tm, tt, dm, dt = (picks[:, i : i + 1] for i in range(4))
    sums = jnp.zeros((queries, LANE), jnp.float32)
    excesses = []
    for o in range(outer):
        t_stop = jnp.exp(chosen(lambda p: ts[o, rows_of(p)]) - tm) / tt
        d_stop = jnp.exp(chosen(lambda p: ds[o, rows_of(p)]) - dm) / dt
        excess = jnp.maximum(t_stop - d_stop, 0.0) + blend_share * t_stop
        sums = sums + excess
        excesses.append(excess)
    sums = jnp.broadcast_to(jnp.sum(sums, axis=1, keepdims=True), (queries, LANE))
    sums = jnp.concatenate([sums, jnp.zeros((LANE - queries, LANE), jnp.float32)], axis=0)
    st_out[2] = jnp.transpose(sums)[0:8]
    spread(2, 0)
    total = st_in[2, 0]
    for j in range(1, 8):
        total = total + st_in[2, j]
    st_out[3] = total
    spread(3, 1)
    total = st_in[3, 0]
    for j in range(1, 8):
        total = total + st_in[3, j]
    total = jnp.concatenate([total, jnp.zeros((LANE - 8, LANE), jnp.float32)], axis=0)
    total = jnp.transpose(total)[0:queries, 0:1]
    for o in range(outer):
        resid_ref[:, o * LANE : (o + 1) * LANE] = (excesses[o] / total).astype(jnp.bfloat16)

    t_log = t_tok - t_max - jnp.log(t_sum)
    d_log = d_tok - d_max - jnp.log(d_sum)
    ratio_ref[...] = jnp.broadcast_to(
        jnp.exp(jnp.minimum(0.0, t_log - d_log)), ratio_ref.shape
    )

    await_bytes(z_in.at[pl.ds(0, 7)], z_send)
    for k, buffer in enumerate((a1, a2, a3)):
        await_bytes(buffer.at[pl.ds(0, 7)], a_send.at[k])
    for k in range(4):
        await_bytes(st_in.at[k, pl.ds(0, 7)], st_send.at[k])
    for direction in (0, 1):
        for t in range(4):
            piece = mine(y) if t < 3 else sub(y, direction)
            await_bytes(piece, y_send.at[direction, t])
    for k in range(8):
        await_bytes(mine(y), sib_send.at[k])
    for t in range(1, 8):
        yy = (b + t) % 8
        for h in (0, 1):
            await_bytes(part.at[yy, h], p_send.at[yy, h])


def per_device(
    latent_states,
    unembedding_weights,
    drafter_raw_scores,
    sampler_heat,
    drafter_guesses,
    first_refused_slot,
):
    depth = latent_states.shape[2]
    outer = unembedding_weights.shape[1]
    columns = outer * LANE
    chunks = depth // LANE
    queries = sampler_heat.shape[0]
    rows = queries * POS
    own = latent_states.reshape(REQ, POS, chunks, LANE).transpose(1, 2, 0, 3)
    weights = unembedding_weights.reshape(depth, outer, LANE)
    draft = drafter_raw_scores.reshape(REQ, POS, RING_Y, GROUP, LANE).transpose(2, 3, 1, 0, 4)
    steps = lax.broadcasted_iota(jnp.int32, (POS, queries), 0)
    meta = jnp.stack(
        [
            jnp.broadcast_to(sampler_heat[None, :], (POS, queries)),
            drafter_guesses.T.astype(jnp.float32),
            (steps == first_refused_slot[None, :]).astype(jnp.float32),
        ],
        axis=-1,
    ).reshape(rows, 3)
    meta = jnp.pad(meta, ((0, 0), (0, LANE - 3)))
    f32, bf16 = jnp.float32, jnp.bfloat16
    dma = pltpu.SemaphoreType.DMA
    half = columns // 2
    ratio, residual = pl.pallas_call(
        kernel,
        out_shape=(
            jax.ShapeDtypeStruct((8, LANE), f32),
            jax.ShapeDtypeStruct((queries, columns), bf16),
        ),
        in_specs=[
            pl.BlockSpec(memory_space=pltpu.VMEM),
            pl.BlockSpec(memory_space=pl.ANY),
            pl.BlockSpec(memory_space=pltpu.VMEM),
            pl.BlockSpec(memory_space=pltpu.VMEM),
        ],
        out_specs=(
            pl.BlockSpec(memory_space=pltpu.VMEM),
            pl.BlockSpec(memory_space=pltpu.VMEM),
        ),
        scratch_shapes=[
            pltpu.VMEM((depth, outer, LANE), bf16),
            pltpu.VMEM((depth, columns), bf16),
            pltpu.VMEM((GROUP, POS, chunks // 2, REQ, LANE), bf16),
            pltpu.VMEM((RING_Y, chunks, rows, LANE), bf16),
            pltpu.VMEM((RING_Y, 2, rows, half), f32),
            pltpu.VMEM((RING_Y, rows, half), f32),
            pltpu.VMEM((2, 2, 2, rows, half), f32),
            pltpu.VMEM((2, rows, half), f32),
            pltpu.VMEM((GROUP, RING_Y, POS, REQ, LANE), bf16),
            pltpu.VMEM((RING_Y, GROUP, POS, REQ, LANE), bf16),
            pltpu.VMEM((8, GROUP, POS, REQ, LANE), bf16),
            pltpu.VMEM((outer, rows, LANE), f32),
            pltpu.VMEM((outer, rows, LANE), f32),
            pltpu.VMEM((4, 8, LANE), f32),
            pltpu.VMEM((4, 8, 8, LANE), f32),
            dma,
            dma,
            dma,
            dma((2, 4)),
            dma((2, 4)),
            dma((8,)),
            dma((8,)),
            dma((8, 2)),
            dma((8,)),
            dma((2, 2, 2)),
            dma((2,)),
            dma((3,)),
            dma((3,)),
            dma((4,)),
            dma((4,)),
        ],
        compiler_params=pltpu.CompilerParams(
            collective_id=0, has_side_effects=True, vmem_limit_bytes=48 << 20
        ),
    )(own, weights, draft, meta)
    ratio = ratio[0, :rows].reshape(POS, queries).T
    residual = residual.reshape(queries, outer, 1, LANE)
    return ratio, residual


def solution(mesh):
    in_specs = (
        P("vocab", None, "batch"),
        P("batch", None, "vocab", None),
        P("vocab", None, "batch", None, None),
        P("batch"),
        P("batch", None),
        P("batch"),
    )
    out_specs = (P("batch", None), P("batch", None, "vocab", None))
    return jax.shard_map(
        per_device, mesh=mesh, in_specs=in_specs, out_specs=out_specs, check_vma=False
    )
```

time: 681 us -> 101 us (0.15)
  blocking collectives: 411 us -> 0 us
  waiting for transfers between devices: 220 us -> 0 us
  Pallas kernels: 0 us -> 92.2 us
  starting transfers between devices: 14.2 us -> 0 us
  between operations: 14.2 us -> 0.66 us
    psum x2 -> x0, blocking collectives: 274 us -> none  [the longest x1 137 us: per_device(): lax.psum((target_hit, draft_hit, jnp.sum(excess, axis=-1)), 'vocab')]
    pmax x1 -> x0, blocking collectives: 137 us -> none  [per_device(): lax.pmax((jnp.max(target_scores, axis=-1), jnp.max(draft_scores, axis=-1)...]
    all_gather x1 -> x0, waiting for transfers between devices: 128 us -> none  [per_device(): gathered = lax.all_gather(latent_states, 'vocab', axis=0, tiled=True)]
    pallas_call x0 -> x1, Pallas kernels: none -> 92.2 us  [per_device(): pl.pallas_call(kernel, out_shape=(jax.ShapeDtypeStruct((8, LANE), f32), j...]
    reduce_scatter x1 -> x0, waiting for transfers between devices: 68.6 us -> none  [per_device(): lax.psum_scatter(jnp.dot(every_row, weight_block, preferred_element_type=...]
    all_to_all x2 -> x0, waiting for transfers between devices: 23.4 us -> none  [the longest x1 12.6 us: per_device(): lax.all_to_all(drafter_raw_scores, 'vocab', split_axis=3, concat_axis=0,...]
    all_to_all x2 -> x0, starting transfers between devices: 14.1 us -> none  [the longest x1 7.1 us: per_device(): lax.all_to_all(drafter_raw_scores, 'vocab', split_axis=3, concat_axis=0,...]
  transfers between devices with their start and end apart: 4 -> 0, of which waited for: 4 -> 0; matrix products, arithmetic and copies ran while one was open for 0% -> 0% of each run, Pallas kernels for 0% -> 0%
where the time goes in v1:
time: 101 us
  Pallas kernels  92.2 us (91%)
  local copies, waits for them, and re-layouts  7.11 us (7%)
    pallas_call x1, Pallas kernels, per_device(): pl.pallas_call(kernel, out_shape=(jax.ShapeDtypeStruct((8, LANE), f32), j...  92.2 us
    unnamed x6, local copies, waits for them, and re-layouts  4.67 us

profile of v1, /device:TPU:1, one launch (start us, length us, event | category | flops | bytes accessed | tf_op | source)
XLA Modules:
  0.0 100.7 jit_solution(5575076737692343763)
XLA Ops:
  0.6 0.7 stack_broadcast_in_dim.7
  1.3 0.1 stack_broadcast_in_dim.8
  1.4 0.7 convert_bitcast_fusion
  2.1 0.1 stack.7
  2.1 0.7 eq.18
  2.8 0.1 eq.19
  2.9 0.1 iota.8
  3.0 0.1 copy.21
  3.1 1.1 %copy.20 = bf16[2,5,1,64,128]{4,0,1,3,2:T(2,128)(2,1)S(1)} copy(bf16[2,5,1,64,128]{4,3,2,1,0:T(8,128)(2,1)} %param.8) | data formatting | bytes 327680 | tf_op args[2]
  4.2 0.0 copy-start
  4.2 2.2 %copy-done = bf16[2048,8,1,128]{3,1,2,0:T(8,128)(2,1)S(1)} copy-done((bf16[2048,8,1,128]{3,1,2,0:T(8,128)(2,1)S(1)}, bf16[2048,8,1,128]{3,1,2,0:T(8,128)(2,1)}, u32[]{:S(2)}) %copy-start) | copy-done | bytes 4194328
  6.4 0.0 copy-start.1
  6.4 0.8 copy-done.1
  7.2 92.2 %shard_map.77 = (f32[8,128]{1,0:T(8,128)S(1)}, bf16[16,1024]{1,0:T(8,128)(2,1)S(1)}) custom-call(bf16[5,16,2,128]{3,2,1,0:T(2,128)(2,1)S(1)} %bitcast.20, bf16[2048,8,128]{2,1,0:T(8,128)(2,1)S(1)} %bitcast.18, bf16[8,8,5,2,128]{4,3,2,1,0:T(2,128)(2,1)S(1)} %bitcast.19, f32[80,128]{1,0:T(8,128)S(1)} %pad.4.meta_ref), custom_call_target="tpu_custom_call" | custom-call | tf_op jit(solution)/shard_map/pallas_call | solution.py:507
  99.4 0.6 copy.23
  100.0 0.7 reshape_squeeze.3
  (5 shorter events, 0.0 us)
Async XLA Ops:
  4.2 2.2 %copy-start = (bf16[2048,8,1,128]{3,1,2,0:T(8,128)(2,1)S(1)}, bf16[2048,8,1,128]{3,1,2,0:T(8,128)(2,1)}, u32[]{:S(2)}) copy-start(bf16[2048,8,1,128]{3,1,2,0:T(8,128)(2,1)} %param.7) | copy-start | bytes 12582916
  6.4 0.8 copy-start.1
